TPU v7x, 32 devices: a whole 2x2x4 slice. The times are simulated.
32 devices in a mesh: depth: 8 (over z, x), lat: 4 (over y, core).
Axes of the slice: x: 2, y: 2, z: 4, core: 2. Of those that a mesh axis runs over, the one named last changes fastest.
Arguments:
- phase: float32 [256, 256, 128], P('depth', 'lat'), may hold values from 0 to 1
- temper: float32 [256, 256, 128], P('depth', 'lat'), may hold values from -3 to 3
- iface_count: int32 [8, 4], P('depth', 'lat'), may hold values from 1 to 32, as said below
Outputs:
- phase_next: float32 [256, 256, 128], P('depth', 'lat')
- heat_next: float32 [256, 256, 128], P('depth', 'lat')
- picture: float32 [4, 256, 512], P(None, 'lat', 'depth')
Inputs may be any that keep to these rules, and one draw needn't show every extreme that they name: `iface_count`: per brick a count of 1 to 32; some brick has exactly 32 and another exactly 1.
All inputs are finite; a program needn't handle non-finite values.
Results may differ from a plain program's by a relative error of at most 0.0003.
Values sent between devices are 32-bit elements; how exact they have to be, the bound alone decides.
A program may use at most 64 MiB of HBM per device.

v0:
```python
import functools
import math

import jax
import jax.numpy as jnp
import numpy as np
from jax import lax
from jax.experimental import pallas as pl
from jax.experimental.pallas import tpu as pltpu
from jax.sharding import PartitionSpec as P

SWEEPS = 3

DIFFUSION = (0.5, 2.0)
TIME_STEP = 0.4
COUPLE = 0.6
LATENT = 0.5
SHEAR_Y = (1.6, -1.6, 0.8, -1.2)
SHEAR_Z = (0.9, -0.6, -0.9, 0.3)
CENTERS = (-0.8, 0.0, 0.8)
VIEWS = len(SHEAR_Y)
MESH = pl.DeviceIdType.MESH
TILE = 8
REACH = 4
GROUPS = 4
WINDOW = 4
CHUNKS = 8
STEP = 8
EARLY = 1


def thetas(sweep_total):
    chebyshev = []
    for f in range(2):
        highest = 1.0 + 12.0 * DIFFUSION[f]
        entries = [
            0.5 * (highest + 1.0)
            + 0.5 * (highest - 1.0) * math.cos((2 * j + 1) * math.pi / (2 * sweep_total))
            for j in range(sweep_total)
        ]
        chebyshev.append(entries)
    return np.array(chebyshev)


def over(front, behind):
    return [front[c] + front[3] * behind[c] for c in range(3)] + [front[3] * behind[3]]


def segments(x_lo, x_hi, shear, layers):
    runs = []
    for x in range(x_lo, x_hi):
        whole = int(math.floor(abs(shear) * x / layers))
        if runs and runs[-1][2] == whole:
            runs[-1][1] = x + 1
        else:
            runs.append([x, x + 1, whole])
    return runs


def blocked(lo, hi, step, body, carry):
    count = (hi - lo) // step

    def block(i, inner):
        return body([lo + i * step + j for j in range(step)], inner)

    if count:
        carry = lax.fori_loop(0, count, block, carry)
    rest = list(range(lo + count * step, hi))
    return body(rest, carry) if rest else carry


def kernel(
    depth_size,
    lat_size,
    swap,
    phase_ref,
    temper_ref,
    count_ref,
    phase_out,
    heat_out,
    picture_ref,
    u0,
    u1,
    u2,
    u3,
    src,
    stash,
    keep,
    sent,
    xrecv,
    merged,
    zrecv,
    in_sem,
    out_sem,
    xs_sem,
    xr_sem,
    ys_sem,
    yr_sem,
    cs_sem,
    cr_sem,
    ps_sem,
    pr_sem,
    zs_sem,
    zr_sem,
):
    layers, rows, cols = phase_ref.shape
    halo = SWEEPS
    d = lax.axis_index("depth")
    l = lax.axis_index("lat")
    has_prev, has_next = d > 0, d < depth_size - 1
    has_low, has_high = l > 0, l < lat_size - 1
    up, down = lax.rem(d + 1, depth_size), lax.rem(d + depth_size - 1, depth_size)
    right, left = lax.rem(l + 1, lat_size), lax.rem(l + lat_size - 1, lat_size)
    xbit = lax.rem(d, 2)
    myz = d // 2
    partner = d + 1 - 2 * xbit
    fields = (phase_ref, temper_ref)

    local = [
        pltpu.make_async_copy(
            fields[f], u0.at[f, pl.ds(halo, layers), pl.ds(TILE, rows), :], in_sem.at[f]
        )
        for f in range(2)
    ]
    for copy in local:
        copy.start()

    barrier = pltpu.get_barrier_semaphore()
    greet = ((has_prev, (down, l)), (has_next, (up, l)), (has_low, (d, left)), (has_high, (d, right)))
    for there, device in greet:

        @pl.when(there)
        def _():
            pl.semaphore_signal(barrier, inc=1, device_id=device, device_id_type=MESH)

    if swap:
        for z in range(VIEWS):

            @pl.when(myz != z)
            def _():
                pl.semaphore_signal(
                    barrier, inc=1, device_id=(2 * z + xbit, l), device_id_type=MESH
                )

    @pl.when(d == 0)
    def _():
        u0[:, :halo] = jnp.zeros((2, halo, rows + 2 * TILE, cols), jnp.float32)

    @pl.when(d == depth_size - 1)
    def _():
        u0[:, halo + layers :] = jnp.zeros((2, halo, rows + 2 * TILE, cols), jnp.float32)

    for edge, first in ((l == 0, 0), (l == lat_size - 1, TILE + rows)):

        @pl.when(edge)
        def _():
            def clear(x, carry):
                for f in range(2):
                    u0[f, x, pl.ds(first, TILE), :] = jnp.zeros((TILE, cols), jnp.float32)
                return carry

            lax.fori_loop(0, layers + 2 * halo, clear, 0)

    peers = sum(
        jnp.minimum(n, 1) for n in (d, depth_size - 1 - d, l, lat_size - 1 - l)
    )
    pl.semaphore_wait(barrier, peers + (VIEWS - 1 if swap else 0))

    lat_copies, edge_copies, mid_copies, corner_copies = [], [], [], []
    groups = GROUPS if layers % GROUPS == 0 else 1
    depth = layers // groups
    for g in range(groups):
        lat_copies.append([])
        for way in range(2):
            row_from, row_to = ((rows - TILE, 0), (0, TILE + rows))[way]
            for f in range(2):
                copy = pltpu.make_async_remote_copy(
                    src_ref=fields[f].at[pl.ds(g * depth, depth), pl.ds(row_from, TILE), :],
                    dst_ref=u0.at[f, pl.ds(halo + g * depth, depth), pl.ds(row_to, TILE), :],
                    send_sem=ys_sem.at[g, way, f],
                    recv_sem=yr_sem.at[g, way, f],
                    device_id=(d, (right, left)[way]),
                    device_id_type=MESH,
                )
                entry = ((has_high, has_low)[way], (has_low, has_high)[way], copy)
                lat_copies[g].append(entry)
    pieces = ((0, TILE), (rows - TILE, TILE), (TILE, rows - 2 * TILE))
    for piece, (row, size) in enumerate(pieces):
        for way in range(2):
            layer_from, layer_to = ((layers - halo, 0), (0, halo + layers))[way]
            for f in range(2):
                copy = pltpu.make_async_remote_copy(
                    src_ref=fields[f].at[pl.ds(layer_from, halo), pl.ds(row, size), :],
                    dst_ref=u0.at[f, pl.ds(layer_to, halo), pl.ds(TILE + row, size), :],
                    send_sem=xs_sem.at[piece, way, f],
                    recv_sem=xr_sem.at[piece, way, f],
                    device_id=((up, down)[way], l),
                    device_id_type=MESH,
                )
                entry = ((has_next, has_prev)[way], (has_prev, has_next)[way], copy)
                (mid_copies if piece == 2 else edge_copies).append(entry)
    for side in range(2):
        layer = (0, halo + layers)[side]
        filled = (has_prev, has_next)[side]
        for way in range(2):
            row_from, row_to = ((rows, 0), (TILE, TILE + rows))[way]
            copy = pltpu.make_async_remote_copy(
                src_ref=u0.at[:, pl.ds(layer, halo), pl.ds(row_from, TILE), :],
                dst_ref=u0.at[:, pl.ds(layer, halo), pl.ds(row_to, TILE), :],
                send_sem=cs_sem.at[side, way],
                recv_sem=cr_sem.at[side, way],
                device_id=(d, (right, left)[way]),
                device_id_type=MESH,
            )
            sends = jnp.logical_and(filled, (has_high, has_low)[way])
            receives = jnp.logical_and(filled, (has_low, has_high)[way])
            corner_copies.append((sends, receives, copy))

    def start(entries):
        for sends, _receives, copy in entries:
            pl.when(sends)(copy.start)

    def arrive(entries):
        for _sends, receives, copy in entries:
            pl.when(receives)(copy.wait_recv)

    def leave(entries):
        for sends, _receives, copy in entries:
            pl.when(sends)(copy.wait_send)

    start(edge_copies)
    start(lat_copies[0])
    start(mid_copies)
    for g in range(1, groups):
        start(lat_copies[g])
    for copy in local:
        copy.wait()

    chebyshev = thetas(SWEEPS)
    first_row = TILE - REACH
    span = rows + 2 * REACH
    chunk = next(n for n in (24, 16, 8) if span % n == 0)
    lane = lax.broadcasted_iota(jnp.int32, (chunk, cols), 1)
    row_id = lax.broadcasted_iota(jnp.int32, (chunk, cols), 0)
    low_mask = jnp.where(jnp.logical_or(row_id >= REACH, has_low), 1.0, 0.0)
    high_mask = jnp.where(jnp.logical_or(row_id < chunk - REACH, has_high), 1.0, 0.0)

    def sweep(k, before, after, x_lo, x_hi, edge):
        def body(xs, carry):
            for x in xs:
                factor = None
                if edge:
                    inside = jnp.logical_and(
                        jnp.logical_or(x >= halo, has_prev),
                        jnp.logical_or(x < halo + layers, has_next),
                    )
                    factor = jnp.where(inside, 1.0, 0.0)
                for r0 in range(first_row, first_row + span, chunk):
                    here = pl.ds(r0, chunk)
                    values = [before[f, x, here, :] for f in range(2)]
                    if k == 0:
                        p, t = values
                        reaction = p * (1.0 - p) * (p - 0.5 + COUPLE * t)
                        sources = [p + TIME_STEP * reaction, t + LATENT * TIME_STEP * reaction]
                    else:
                        sources = [src[f, x, here, :] for f in range(2)]
                    for f in range(2):
                        u = values[f]
                        around = before[f, x - 1, here, :] + before[f, x + 1, here, :]
                        around = around + (
                            before[f, x, pl.ds(r0 - 1, chunk), :]
                            + before[f, x, pl.ds(r0 + 1, chunk), :]
                        )
                        around = around + (
                            jnp.where(lane == 0, 0.0, pltpu.roll(u, 1, 1))
                            + jnp.where(lane == cols - 1, 0.0, pltpu.roll(u, cols - 1, 1))
                        )
                        theta = chebyshev[f, k]
                        new = (
                            float(1.0 - (1.0 + 6.0 * DIFFUSION[f]) / theta) * u
                            + float(1.0 / theta) * sources[f]
                            + float(DIFFUSION[f] / theta) * around
                        )
                        if r0 == first_row:
                            new = new * low_mask
                        if r0 + chunk == first_row + span:
                            new = new * high_mask
                        if edge:
                            new = new * factor
                        after[f, x, here, :] = new
                        if k == 0:
                            src[f, x, here, :] = sources[f]
            return carry

        blocked(x_lo, x_hi, 4, body, 0)

    stages = (u0, u1, u2, u3)
    total = layers + 2 * halo
    ready = halo + 1
    for g in range(groups):
        arrive(lat_copies[g])
        until = halo + (g + 1) * depth - 1
        sweep(0, u0, u1, ready, until, False)
        ready = until
    for k in range(1, SWEEPS):
        sweep(k, stages[k], stages[k + 1], halo + 1 + k, halo + layers - 1 - k, False)

    half = rows // 2
    count = count_ref[0, 0]
    lane1 = lax.broadcasted_iota(jnp.int32, (TILE, cols), 1)
    first_lane, last_lane = lane1 == 0, lane1 == cols - 1
    opacity = 4.0 / (layers * depth_size)
    starts = range(0, half, TILE)

    def render(v, r0, x_lo, x_hi, carry):
        sy = 1 if SHEAR_Y[v] > 0 else -1
        sz = 1 if SHEAR_Z[v] > 0 else -1
        edge_lane = last_lane if sz > 0 else first_lane

        def layer(x, whole, groups):
            xf = lax.convert_element_type(x, jnp.float32)
            fy = xf * (abs(SHEAR_Y[v]) / layers) - whole
            fz = xf * (abs(SHEAR_Z[v]) / layers)
            far_z = jnp.where(edge_lane, 0.0, fz)
            near_z = 1.0 - fz
            scale = jnp.where(x < count, -opacity, 0.0)
            result = []
            for row, (trans, red, green, blue) in zip(starts, groups):
                sampled = []
                for f in range(2):
                    first = TILE + r0 + row
                    near = u3[f, x + halo, pl.ds(first + sy * whole, TILE), :]
                    far = u3[f, x + halo, pl.ds(first + sy * (whole + 1), TILE), :]
                    b = near + fy * (far - near)
                    beside = pltpu.roll(b, cols - 1 if sz > 0 else 1, 1)
                    sampled.append(near_z * b + far_z * beside)
                after = trans * jnp.exp(scale * (sampled[0] * sampled[0]))
                weight = trans - after
                s = sampled[1]
                q = s * s
                d1 = q + 1.0
                a = q + (1.0 + CENTERS[2] * CENTERS[2])
                b = (2.0 * CENTERS[2]) * s
                d0, d2 = a + b, a - b
                result.append(
                    (
                        after,
                        red + weight * pl.reciprocal(d0, approx=True),
                        green + weight * pl.reciprocal(d1, approx=True),
                        blue + weight * pl.reciprocal(d2, approx=True),
                    )
                )
            return result

        groups = [tuple(c[r : r + TILE] for c in carry) for r in starts]
        for lo, hi, whole in segments(x_lo, x_hi, SHEAR_Y[v], layers):

            def body(xs, inner, whole=whole):
                for x in xs:
                    inner = layer(x, whole, inner)
                return inner

            groups = blocked(lo, hi, STEP, body, groups)
        return tuple(jnp.concatenate([g[c] for g in groups], axis=0) for c in range(4))

    zero = jnp.zeros((half, cols), jnp.float32)
    one = jnp.ones((half, cols), jnp.float32)

    start_carry = (one, zero, zero, zero)
    order = [0, VIEWS - 1] + list(range(1, VIEWS - 1))
    units = [(v, h) for v in order for h in range(2)]
    for place in range(EARLY):
        v, h = units[place]
        inner = render(v, h * half, halo, layers - halo, start_carry)
        for c in range(4):
            stash[place, c] = inner[c]

    arrive(edge_copies)
    start(corner_copies)
    arrive(mid_copies)
    arrive(corner_copies)
    for k in range(SWEEPS):
        sweep(k, stages[k], stages[k + 1], 1 + k, halo + 1 + k, True)
        sweep(k, stages[k], stages[k + 1], halo + layers - 1 - k, total - 1 - k, True)

    outs = [
        pltpu.make_async_copy(
            u3.at[f, pl.ds(halo, layers), pl.ds(TILE, rows), :],
            (phase_out, heat_out)[f],
            out_sem.at[f],
        )
        for f in range(2)
    ]
    for copy in outs:
        copy.start()

    def piece_of(place):
        v, h = units[place]
        if place < EARLY:
            trans, *colours = render(v, h * half, 0, halo, start_carry)
            inner = [stash[place, c] for c in range(4)]
            carry = (trans * inner[0],) + tuple(
                colours[c] + trans * inner[1 + c] for c in range(3)
            )
            carry = render(v, h * half, layers - halo, layers, carry)
        else:
            carry = render(v, h * half, 0, layers, start_carry)
        trans, red, green, blue = carry
        return [red, green, blue, trans]

    if not swap:
        for place, (v, h) in enumerate(units):
            part = piece_of(place)
            for c in range(4):
                picture_ref[c, h * half : (h + 1) * half, v * cols : (v + 1) * cols] = part[c]
    else:
        quarter = half // 2
        left_lanes = lax.broadcasted_iota(jnp.int32, (quarter, cols), 1) < cols // 2

        def pair_copy(v, h):
            return pltpu.make_async_remote_copy(
                src_ref=sent.at[v, h],
                dst_ref=xrecv.at[v, h],
                send_sem=ps_sem.at[v, h],
                recv_sem=pr_sem.at[v, h],
                device_id=(partner, l),
                device_id_type=MESH,
            )

        def group_copy(v, h, slot):
            return pltpu.make_async_remote_copy(
                src_ref=merged.at[v, h],
                dst_ref=zrecv.at[slot, h],
                send_sem=zs_sem.at[v, h],
                recv_sem=zr_sem.at[slot, h],
                device_id=(2 * v + xbit, l),
                device_id_type=MESH,
            )

        def send_pair(place):
            v, h = units[place]
            part = piece_of(place)
            for c in range(4):
                lo, hi = part[c][:quarter], part[c][quarter:]
                lower = jnp.where(left_lanes, lo, pltpu.roll(hi, cols // 2, 1))
                upper = jnp.where(left_lanes, pltpu.roll(lo, cols // 2, 1), hi)
                keep[v, h, c] = jnp.where(xbit == 0, lower, upper)
                sent[v, h, c] = jnp.where(xbit == 0, upper, lower)
            pair_copy(v, h).start()

        def send_group(place):
            v, h = units[place]
            pair_copy(v, h).wait_recv()
            mine = [keep[v, h, c] for c in range(4)]
            other = [xrecv[v, h, c] for c in range(4)]
            front = [jnp.where(xbit == 0, m, o) for m, o in zip(mine, other)]
            behind = [jnp.where(xbit == 0, o, m) for m, o in zip(mine, other)]
            result = over(front, behind)

            @pl.when(myz == v)
            def _():
                for c in range(4):
                    zrecv[v, h, c] = result[c]

            @pl.when(myz != v)
            def _():
                for c in range(4):
                    merged[v, h, c] = result[c]
                group_copy(v, h, myz).start()

        for place in range(len(units)):
            send_pair(place)
            if place >= 2:
                send_group(place - 2)
        send_group(len(units) - 2)
        send_group(len(units) - 1)

        for h in range(2):
            for s in range(VIEWS):
                pl.when(myz != s)(group_copy(s, h, s).wait_recv)
            result = [zrecv[VIEWS - 1, h, c] for c in range(4)]
            for s in range(VIEWS - 2, -1, -1):
                result = over([zrecv[s, h, c] for c in range(4)], result)
            for c in range(4):
                picture_ref[h, c] = result[c]
        for v, h in units:
            pair_copy(v, h).wait_send()
            pl.when(myz != v)(group_copy(v, h, myz).wait_send)

    for entries in lat_copies:
        leave(entries)
    leave(edge_copies)
    leave(mid_copies)
    leave(corner_copies)
    for copy in outs:
        copy.wait()


def deliver(phase_ref, heat_ref, packed_ref, phase_out, heat_out, picture_ref, held, into, out):
    layers = phase_ref.shape[0]
    size = layers // CHUNKS
    pairs = ((phase_ref, phase_out), (heat_ref, heat_out))
    arrivals, departures = [], []
    for f, (source, target) in enumerate(pairs):
        for n in range(CHUNKS):
            part = pl.ds(n * size, size)
            arrivals.append(
                pltpu.make_async_copy(source.at[part], held.at[f, part], into.at[f, n])
            )
            departures.append(
                pltpu.make_async_copy(held.at[f, part], target.at[part], out.at[f, n])
            )
    for copy in arrivals[:WINDOW]:
        copy.start()
    halves, channels, quarter, cols = packed_ref.shape
    for h in range(halves):
        for c in range(channels):
            part = packed_ref[h, c]
            first = 2 * h * quarter
            picture_ref[c, first : first + quarter, :] = part[:, : cols // 2]
            picture_ref[c, first + quarter : first + 2 * quarter, :] = pltpu.roll(
                part, cols // 2, 1
            )[:, : cols // 2]
    for n, (arrival, departure) in enumerate(zip(arrivals, departures)):
        arrival.wait()
        departure.start()
        if n + WINDOW < len(arrivals):
            arrivals[n + WINDOW].start()
    for copy in departures:
        copy.wait()


def from_partner(shard, axis, apart):
    return lax.ppermute(shard, axis, [(i, i ^ 1 << apart) for i in range(lax.axis_size(axis))])


def over_blend(in_front, behind):
    return jnp.concatenate(
        [in_front[:3] + in_front[3:] * behind[:3], in_front[3:] * behind[3:]], axis=0
    )


def binary_swap(picture, depth_size):
    row_count, pixels = picture.shape[1:]
    bit_count = depth_size.bit_length() - 1
    block_width = pixels >> bit_count
    shaped = picture.reshape((4, row_count) + (2,) * bit_count + (block_width,))
    permuted = (0, 1) + tuple(range(bit_count + 1, 1, -1)) + (bit_count + 2,)
    picture = jnp.transpose(shaped, permuted).reshape(4, row_count, pixels)
    my_index = lax.axis_index("depth")
    for b in range(bit_count):
        half_width = picture.shape[2] // 2
        front_half = picture[:, :, :half_width]
        second = picture[:, :, half_width:]
        upper_bit = my_index >> b & 1 == 1
        kept_half = jnp.where(upper_bit, second, front_half)
        sent_half = jnp.where(upper_bit, front_half, second)
        partner = from_partner(sent_half, "depth", b)
        in_front = jnp.where(upper_bit, partner, kept_half)
        behind = jnp.where(upper_bit, kept_half, partner)
        picture = over_blend(in_front, behind)
    return picture


def per_device(phase, temper, iface_count):
    layers, rows, cols = phase.shape
    depth_size = lax.axis_size("depth")
    lat_size = lax.axis_size("lat")
    swap = depth_size == 2 * VIEWS
    packed = (2, 4, rows // 4, cols)
    piece = packed if swap else (4, rows, VIEWS * cols)
    grid = (2, layers + 2 * SWEEPS, rows + 2 * TILE, cols)
    tile = (VIEWS,) + packed
    dma = pltpu.SemaphoreType.DMA
    phase_next, heat_next, picture = pl.pallas_call(
        functools.partial(kernel, depth_size, lat_size, swap),
        out_shape=(
            jax.ShapeDtypeStruct(phase.shape, jnp.float32),
            jax.ShapeDtypeStruct(phase.shape, jnp.float32),
            jax.ShapeDtypeStruct(piece, jnp.float32),
        ),
        in_specs=[
            pl.BlockSpec(memory_space=pl.ANY),
            pl.BlockSpec(memory_space=pl.ANY),
            pl.BlockSpec(memory_space=pltpu.SMEM),
        ],
        out_specs=(
            pl.BlockSpec(memory_space=pl.ANY),
            pl.BlockSpec(memory_space=pl.ANY),
            pl.BlockSpec(memory_space=pltpu.VMEM),
        ),
        scratch_shapes=[pltpu.VMEM(grid, jnp.float32) for _ in range(5)]
        + [pltpu.VMEM((EARLY, 4, rows // 2, cols), jnp.float32)]
        + [pltpu.VMEM(tile, jnp.float32) for _ in range(5)]
        + [
            dma((2,)),
            dma((2,)),
            dma((3, 2, 2)),
            dma((3, 2, 2)),
            dma((GROUPS, 2, 2)),
            dma((GROUPS, 2, 2)),
            dma((2, 2)),
            dma((2, 2)),
            dma((VIEWS, 2)),
            dma((VIEWS, 2)),
            dma((VIEWS, 2)),
            dma((VIEWS, 2)),
        ],
        compiler_params=pltpu.CompilerParams(
            collective_id=0, has_side_effects=True, vmem_limit_bytes=60 * 1024 * 1024
        ),
    )(phase, temper, iface_count)
    if not swap:
        return phase_next, heat_next, binary_swap(picture, depth_size)
    return pl.pallas_call(
        deliver,
        out_shape=(
            jax.ShapeDtypeStruct(phase.shape, jnp.float32),
            jax.ShapeDtypeStruct(phase.shape, jnp.float32),
            jax.ShapeDtypeStruct((4, rows, cols // 2), jnp.float32),
        ),
        in_specs=[
            pl.BlockSpec(memory_space=pl.ANY),
            pl.BlockSpec(memory_space=pl.ANY),
            pl.BlockSpec(memory_space=pltpu.VMEM),
        ],
        out_specs=(
            pl.BlockSpec(memory_space=pl.ANY),
            pl.BlockSpec(memory_space=pl.ANY),
            pl.BlockSpec(memory_space=pltpu.VMEM),
        ),
        scratch_shapes=[
            pltpu.VMEM((2,) + phase.shape, jnp.float32),
            dma((2, CHUNKS)),
            dma((2, CHUNKS)),
        ],
        compiler_params=pltpu.CompilerParams(vmem_limit_bytes=60 * 1024 * 1024),
    )(phase_next, heat_next, picture)


def solution(mesh):
    return jax.shard_map(
        per_device,
        mesh=mesh,
        in_specs=(P("depth", "lat", None), P("depth", "lat", None), P("depth", "lat")),
        out_specs=(P("depth", "lat", None), P("depth", "lat", None), P(None, "lat", "depth")),
        check_vma=False,
    )
```

profile of v0, /device:TPU:20, one launch (start us, length us, event | category | flops | bytes accessed | tf_op | source)
XLA Modules:
  0.0 40.8 jit_solution(9294076886111111707)
XLA Ops:
  1.3 32.7 %shard_map.58 = (f32[32,64,128]{2,1,0:T(8,128)}, f32[32,64,128]{2,1,0:T(8,128)}, f32[2,4,16,128]{3,2,1,0:T(8,128)}) custom-call(f32[32,64,128]{2,1,0:T(8,128)} %phase_ref.1, f32[32,64,128]{2,1,0:T(8,128)} %temper_ref.1, s32[1,1]{1,0:T(1,128)S(6)} %copy.6.count_ref), custom_call_target="tpu_custom_call" | custom-call | tf_op jit(solution)/shard_map/pallas_call | solution.py:575
  34.0 6.8 %shard_map.59 = (f32[32,64,128]{2,1,0:T(8,128)}, f32[32,64,128]{2,1,0:T(8,128)}, f32[4,64,64]{2,1,0:T(8,128)}) custom-call(f32[32,64,128]{2,1,0:T(8,128)} %get-tuple-element.6.phase_ref, f32[32,64,128]{2,1,0:T(8,128)} %get-tuple-element.7.heat_ref, f32[2,4,16,128]{3,2,1,0:T(8,128)} %get-tuple-element.8.packed_ref), custom_call_target="tpu_custom_call" | custom-call | tf_op jit(solution)/shard_map/pallas_call | solution.py:615
where the time goes:
time: 41.1 us; the launch traced here: 40.8 us
  Pallas kernels  39.5 us (96%)
  between operations  1.28 us (3%)
    pallas_call x1, Pallas kernels, per_device(): pl.pallas_call(functools.partial(kernel, depth_size, lat_size, swap), out...  32.7 us
    pallas_call x1, Pallas kernels, per_device(): pl.pallas_call(deliver, out_shape=(jax.ShapeDtypeStruct(phase.shape, jnp....  6.78 us

commit v1 on v0

--- a/solution.py
+++ b/solution.py
@@ -23,8 +23,7 @@
 TILE = 8
 REACH = 4
 GROUPS = 4
-WINDOW = 4
-CHUNKS = 8
+CHUNKS = 4
 STEP = 8
 EARLY = 1
 
@@ -510,7 +509,7 @@
             departures.append(
                 pltpu.make_async_copy(held.at[f, part], target.at[part], out.at[f, n])
             )
-    for copy in arrivals[:WINDOW]:
+    for copy in arrivals:
         copy.start()
     halves, channels, quarter, cols = packed_ref.shape
     for h in range(halves):
@@ -521,11 +520,9 @@
             picture_ref[c, first + quarter : first + 2 * quarter, :] = pltpu.roll(
                 part, cols // 2, 1
             )[:, : cols // 2]
-    for n, (arrival, departure) in enumerate(zip(arrivals, departures)):
+    for arrival, departure in zip(arrivals, departures):
         arrival.wait()
         departure.start()
-        if n + WINDOW < len(arrivals):
-            arrivals[n + WINDOW].start()
     for copy in departures:
         copy.wait()
 

time: 41.1 us -> 38.1 us (0.927)
  Pallas kernels: 39.5 us -> 36.6 us
    pallas_call x1, Pallas kernels: 6.78 us -> 3.89 us  [per_device(): pl.pallas_call(deliver, out_shape=(jax.ShapeDtypeStruct(phase.shape, jnp....]
where the time goes in v1:
time: 38.1 us; the launch traced here: 37.9 us
  Pallas kernels  36.6 us (96%)
  between operations  1.28 us (3%)
    pallas_call x1, Pallas kernels, per_device(): pl.pallas_call(functools.partial(kernel, depth_size, lat_size, swap), out...  32.7 us
    pallas_call x1, Pallas kernels, per_device(): pl.pallas_call(deliver, out_shape=(jax.ShapeDtypeStruct(phase.shape, jnp....  3.89 us

profile of v1, /device:TPU:20, one launch (start us, length us, event | category | flops | bytes accessed | tf_op | source)
XLA Modules:
  0.0 37.9 jit_solution(5898516555964911939)
XLA Ops:
  1.3 32.7 %shard_map.58 = (f32[32,64,128]{2,1,0:T(8,128)}, f32[32,64,128]{2,1,0:T(8,128)}, f32[2,4,16,128]{3,2,1,0:T(8,128)}) custom-call(f32[32,64,128]{2,1,0:T(8,128)} %phase_ref.1, f32[32,64,128]{2,1,0:T(8,128)} %temper_ref.1, s32[1,1]{1,0:T(1,128)S(6)} %copy.6.count_ref), custom_call_target="tpu_custom_call" | custom-call | tf_op jit(solution)/shard_map/pallas_call | solution.py:572
  34.0 3.9 %shard_map.59 = (f32[32,64,128]{2,1,0:T(8,128)}, f32[32,64,128]{2,1,0:T(8,128)}, f32[4,64,64]{2,1,0:T(8,128)}) custom-call(f32[32,64,128]{2,1,0:T(8,128)} %get-tuple-element.6.phase_ref, f32[32,64,128]{2,1,0:T(8,128)} %get-tuple-element.7.heat_ref, f32[2,4,16,128]{3,2,1,0:T(8,128)} %get-tuple-element.8.packed_ref), custom_call_target="tpu_custom_call" | custom-call | tf_op jit(solution)/shard_map/pallas_call | solution.py:612
